TPU v7x, 32 devices: a whole 2x2x4 slice. The times are simulated.
32 devices in a mesh: ty: 8 (over z, x), tx: 4 (over y, core).
Axes of the slice: x: 2, y: 2, z: 4, core: 2. Of those that a mesh axis runs over, the one named last changes fastest.
Arguments:
- fixed_image: float32 [512, 1024], P('ty', 'tx'), may hold values from -6 to 6
- moving_image: float32 [512, 1024], P('ty', 'tx'), may hold values from -6 to 6
- tissue: int32 [16, 32], P('ty', 'tx'), may hold values from 0 to 1, as said below
Outputs:
- coefficients: float32 [2, 16, 32], P(None, 'ty', 'tx')
- mismatch: float32 [512, 1024], P('ty', 'tx')
Inputs may be any that keep to these rules, and one draw needn't show every extreme that they name: 1 marks a block of 32 x 32 fine pixels that holds tissue, 0 background.
All inputs are finite; a program needn't handle non-finite values.
Results may differ from a plain program's by a relative error of at most 0.0003.
Values sent between devices are 32-bit elements; how exact they have to be, the bound alone decides.
A program may use at most 64 MiB of HBM per device.

v0:
```python
import jax
import jax.numpy as jnp
from jax import lax
from jax.sharding import PartitionSpec as P

SPACE = 32
HALO = 6
MB = 32
ITERS = 2
offset_pairs = (
    (0, 2),
    (0, -2),
    (2, 0),
    (-2, 0),
    (2, 2),
    (2, -2),
    (-2, 2),
    (-2, -2),
    (0, 4),
    (0, -4),
    (4, 0),
    (-4, 0),
)
highest = lax.Precision.HIGHEST


def with_halo(block, sides, width):
    for axis, dim in sides:
        count = lax.axis_size(axis)
        forward = [(i, i + 1) for i in range(count - 1)]
        backward = [(target, source) for source, target in forward]
        low = lax.ppermute(
            lax.slice_in_dim(block, block.shape[dim] - width, None, axis=dim), axis, forward
        )
        high = lax.ppermute(lax.slice_in_dim(block, 0, width, axis=dim), axis, backward)
        block = jnp.concatenate([low, block, high], axis=dim)
    return block


def bspline(values):
    magnitude = jnp.abs(values)
    near_part = 2.0 / 3.0 - magnitude * magnitude + 0.5 * magnitude**3
    far_part = (2.0 - magnitude) ** 3 / 6.0
    return jnp.where(
        magnitude < 1.0, near_part, jnp.where(magnitude < 2.0, far_part, 0.0 * magnitude)
    )


def box_mean(values):
    height, breadth = values.shape
    total = values[0 : height - 2, 0 : breadth - 2]
    for shift_y in range(3):
        for shift_x in range(3):
            if shift_y + shift_x > 0:
                total = (
                    total + values[shift_y : height - 2 + shift_y, shift_x : breadth - 2 + shift_x]
                )
    return total / 9.0


def descriptors(padded):
    height, breadth = padded.shape
    centre = padded[4 : height - 4, 4 : breadth - 4]
    distances = []
    for offset_y, offset_x in offset_pairs:
        shifted = padded[
            4 + offset_y : height - 4 + offset_y, 4 + offset_x : breadth - 4 + offset_x
        ]
        distances.append(box_mean((centre - shifted) ** 2))
    variance = sum(distances) / 12.0 + 0.1
    return [jnp.exp(-member / variance) for member in distances]


def level_terms(fixed_padded, moving_padded, factor):
    fixed_mind = descriptors(fixed_padded)
    moving_mind = descriptors(moving_padded)
    summed = None
    for fixed_part, moving_part in zip(fixed_mind, moving_mind):
        differ = moving_part[1:-1, 1:-1] - fixed_part[1:-1, 1:-1]
        slope_y = (moving_part[2:, 1:-1] - moving_part[:-2, 1:-1]) / (2.0 * factor)
        slope_x = (moving_part[1:-1, 2:] - moving_part[1:-1, :-2]) / (2.0 * factor)
        parts = (
            differ * slope_y,
            differ * slope_x,
            slope_y * slope_y,
            slope_y * slope_x,
            slope_x * slope_x,
            differ * differ,
        )
        summed = (
            parts if summed is None else tuple((left + right for left, right in zip(summed, parts)))
        )
    return summed


def window_matrix(length, factor, cell_count):
    position = factor * jnp.arange(length, dtype=jnp.float32) + (factor - 1) / 2.0
    knots = jnp.arange(cell_count + 3, dtype=jnp.float32) - 1.0
    return bspline(position[:, None] / SPACE - knots[None, :])


def expand_mask(tissue, factor):
    side = MB // factor
    block_rows, block_cols = tissue.shape
    spread = jnp.broadcast_to(
        tissue.astype(jnp.float32)[:, None, :, None], (block_rows, side, block_cols, side)
    )
    return spread.reshape(block_rows * side, block_cols * side)


def pool_stack(images):
    planes, height, breadth = images.shape
    return images.reshape(planes, height // 2, 2, breadth // 2, 2).mean(axis=(2, 4))


def sandwich(left, values, right):
    return jnp.einsum("pa,cab,qb->cpq", left, values, right, precision=highest)


def gradient_terms(summed, weight, field):
    return jnp.stack(
        [
            weight * (summed[0] + summed[2] * field[0] + summed[3] * field[1]),
            weight * (summed[1] + summed[3] * field[0] + summed[4] * field[1]),
        ]
    )


def curvature_density(summed, weight, motion):
    return weight * (
        motion[0] * (summed[2] * motion[0] + summed[3] * motion[1])
        + motion[1] * (summed[3] * motion[0] + summed[4] * motion[1])
    )


def mismatch_of(summed, field):
    return (
        summed[5]
        + 2.0 * (summed[0] * field[0] + summed[1] * field[1])
        + field[0] * (summed[2] * field[0] + summed[3] * field[1])
        + field[1] * (summed[3] * field[0] + summed[4] * field[1])
    )


def window_of(control):
    padded = with_halo(control, (("ty", 1), ("tx", 2)), 2)
    return padded[:, 1:, 1:]


def fold_rim(padded, along, length):
    own_part = lax.slice_in_dim(padded, 4, 4 + length, axis=along)
    from_above = lax.slice_in_dim(padded, 1, 3, axis=along)
    from_below = lax.slice_in_dim(padded, length + 6, length + 7, axis=along)
    above_widths = [(0, 0), (0, 0), (0, 0)]
    above_widths[along] = (0, length - 2)
    below_widths = [(0, 0), (0, 0), (0, 0)]
    below_widths[along] = (length - 1, 0)
    return own_part + jnp.pad(from_above, above_widths) + jnp.pad(from_below, below_widths)


def run_level(padded, weight, coefficients, factor, start_zero):
    summed = level_terms(padded[0], padded[1], factor)
    height, breadth = summed[0].shape
    cells_y = height * factor // SPACE
    cells_x = breadth * factor // SPACE
    rows_window = window_matrix(height, factor, cells_y)
    cols_window = window_matrix(breadth, factor, cells_x)
    if start_zero:
        field = jnp.zeros((2, height, breadth), jnp.float32)
    else:
        field = sandwich(rows_window, window_of(coefficients), cols_window)
    for iteration in range(ITERS):
        pixel_grad = gradient_terms(summed, weight, field)
        partial_grad = sandwich(rows_window.T, pixel_grad, cols_window.T)
        spilled = with_halo(partial_grad, (("ty", 1), ("tx", 2)), 3)
        direction = fold_rim(fold_rim(spilled, 1, cells_y), 2, cells_x)
        motion = sandwich(rows_window, window_of(direction), cols_window)
        norm_sum, curvature = lax.psum(
            (jnp.sum(direction * direction), jnp.sum(curvature_density(summed, weight, motion))),
            ("ty", "tx"),
        )
        step_size = norm_sum / curvature
        coefficients = coefficients - step_size * direction
        field = field - step_size * motion
    return (coefficients, field, summed)


def shards(fixed_image, moving_image, tissue):
    stacked = jnp.stack([fixed_image, moving_image])
    fine_padded = with_halo(stacked, (("ty", 1), ("tx", 2)), HALO)
    coarse_padded = with_halo(pool_stack(stacked), (("ty", 1), ("tx", 2)), HALO)
    cells_y = fixed_image.shape[0] // SPACE
    cells_x = fixed_image.shape[1] // SPACE
    coefficients = jnp.zeros((2, cells_y, cells_x), jnp.float32)
    coefficients, field, summed = run_level(
        coarse_padded, expand_mask(tissue, 2), coefficients, 2, True
    )
    coefficients, field, summed = run_level(
        fine_padded, expand_mask(tissue, 1), coefficients, 1, False
    )
    return (coefficients, mismatch_of(summed, field))


def solution(mesh):
    placed = (P("ty", "tx"), P("ty", "tx"), P("ty", "tx"))
    return jax.shard_map(
        shards,
        mesh=mesh,
        in_specs=placed,
        out_specs=(P(None, "ty", "tx"), P("ty", "tx")),
        check_vma=False,
    )
```

profile of v0, /device:TPU:0, one launch (start us, length us, event | category | flops | bytes accessed | tf_op | source)
XLA Modules:
  0.0 384.1 jit_solution(11618381650321247970)
XLA Ops:
  0.6 6.3 %stack.52 = f32[1,32,2,128,2]{4,3,2,1,0:T(8,128)} reshape(f32[64,256]{1,0:T(8,128)} %param.4) | data formatting | bytes 131072 | tf_op jit(solution)/shard_map/stack | solution.py:189
  7.0 2.8 copy.6
  9.8 5.6 %stack.51 = f32[1,32,2,128,2]{4,3,2,1,0:T(8,128)} reshape(f32[64,256]{1,0:T(8,128)S(1)} %copy-done.1) | data formatting | bytes 131072 | tf_op jit(solution)/shard_map/stack | solution.py:189
  15.4 2.8 copy.5
  19.6 5.5 %collective-permute-start = (f32[2,6,128]{2,1,0:T(8,128)S(1)}, f32[2,6,128]{2,1,0:T(8,128)S(1)}, u32[]{:S(2)}, u32[]{:S(2)}) collective-permute-start(f32[2,6,128]{2,1,0:T(8,128)S(1)} %get-tuple-element.180), channel_id=1, source_target_pairs={{0,4},{4,8},{8,12},{12,16},{16,20},{20,24},{24,28},{1,5},{5,9},{9,... | collective-permute-start | bytes 18440 | tf_op jit(solution)/shard_map/ppermute | solution.py:32
  27.8 3.0 collective-permute-start.2
  36.6 5.4 %collective-permute-start.4 = (f32[2,3,11]{2,1,0:T(4,128)S(1)}, f32[2,3,11]{2,1,0:T(4,128)S(1)}, u32[]{:S(2)}, u32[]{:S(2)}) collective-permute-start(f32[2,3,11]{2,1,0:T(4,128)S(1)} %get-tuple-element.206), channel_id=1, source_target_pairs={{0,4},{4,8},{8,12},{12,16},{16,20},{20,24},{24,28},{1,5},{5,9},{9,... | collective-permute-start | bytes 800 | tf_op jit(solution)/shard_map/ppermute | solution.py:32
  44.7 3.1 collective-permute-start.6
  50.9 5.7 %collective-permute-start.8 = (f32[2,2,8]{2,1,0:T(2,128)S(1)}, f32[2,2,8]{2,1,0:T(2,128)S(1)}, u32[]{:S(2)}, u32[]{:S(2)}) collective-permute-start(f32[2,2,8]{2,1,0:T(2,128)S(1)} %get-tuple-element.36), channel_id=1, source_target_pairs={{0,4},{4,8},{8,12},{12,16},{16,20},{20,24},{24,28},{1,5},{5,9},{9,... | collective-permute-start | bytes 392 | tf_op jit(solution)/shard_map/ppermute | solution.py:32
  59.2 4.9 %collective-permute-start.10 = (f32[2,6,2]{2,1,0:T(8,128)S(1)}, f32[2,6,2]{2,1,0:T(8,128)S(1)}, u32[]{:S(2)}, u32[]{:S(2)}) collective-permute-start(f32[2,6,2]{2,1,0:T(8,128)S(1)} %get-tuple-element.204), channel_id=1, source_target_pairs={{0,1},{1,2},{2,3},{4,5},{5,6},{6,7},{8,9},{9,10},{10,11},{12,13},{... | collective-permute-start | bytes 296 | tf_op jit(solution)/shard_map/ppermute | solution.py:32
  66.1 47.5 %all-reduce.15 = (f32[]{:T(128)}, f32[]{:T(128)}) all-reduce(f32[]{:T(128)} %get-tuple-element.35, f32[]{:T(128)} %multiply_reduce_fusion.3), channel_id=1, replica_groups=mesh['ty'=8,'tx'=4] {'ty','tx'}, use_global_device_ids=true, to_apply=%region_2.3 | all-reduce | flops 2 | bytes 16 | tf_op jit(solution)/shard_map/psum | solution.py:178
  116.7 4.8 %collective-permute-start.12 = (f32[2,3,11]{2,1,0:T(4,128)S(1)}, f32[2,3,11]{2,1,0:T(4,128)S(1)}, u32[]{:S(2)}, u32[]{:S(2)}) collective-permute-start(f32[2,3,11]{2,1,0:T(4,128)S(1)} %get-tuple-element.202), channel_id=1, source_target_pairs={{0,4},{4,8},{8,12},{12,16},{16,20},{20,24},{24,28},{1,5},{5,9},{9,... | collective-permute-start | bytes 800 | tf_op jit(solution)/shard_map/ppermute | solution.py:32
  122.9 5.5 %collective-permute-start.20 = (f32[2,6,256]{2,1,0:T(8,128)S(1)}, f32[2,6,256]{2,1,0:T(8,128)S(1)}, u32[]{:S(2)}, u32[]{:S(2)}) collective-permute-start(f32[2,6,256]{2,1,0:T(8,128)S(1)} %get-tuple-element.102), channel_id=1, source_target_pairs={{0,4},{4,8},{8,12},{12,16},{16,20},{20,24},{24,28},{1,5},{5,9},{9,... | collective-permute-start | bytes 36872 | tf_op jit(solution)/shard_map/ppermute | solution.py:32
  129.7 3.0 collective-permute-start.14
  135.8 5.4 %collective-permute-start.16 = (f32[2,2,8]{2,1,0:T(2,128)S(1)}, f32[2,2,8]{2,1,0:T(2,128)S(1)}, u32[]{:S(2)}, u32[]{:S(2)}) collective-permute-start(f32[2,2,8]{2,1,0:T(2,128)S(1)} %get-tuple-element.34), channel_id=1, source_target_pairs={{0,4},{4,8},{8,12},{12,16},{16,20},{20,24},{24,28},{1,5},{5,9},{9,... | collective-permute-start | bytes 392 | tf_op jit(solution)/shard_map/ppermute | solution.py:32
  143.9 3.4 collective-permute-start.18
  149.3 46.0 %all-reduce.14 = (f32[]{:T(128)}, f32[]{:T(128)}) all-reduce(f32[]{:T(128)} %get-tuple-element.33, f32[]{:T(128)} %multiply_reduce_fusion.2), channel_id=1, replica_groups=mesh['ty'=8,'tx'=4] {'ty','tx'}, use_global_device_ids=true, to_apply=%region_6.7 | all-reduce | flops 2 | bytes 16 | tf_op jit(solution)/shard_map/psum | solution.py:178
  198.0 4.8 %collective-permute-start.24 = (f32[2,2,8]{2,1,0:T(2,128)S(1)}, f32[2,2,8]{2,1,0:T(2,128)S(1)}, u32[]{:S(2)}, u32[]{:S(2)}) collective-permute-start(f32[2,2,8]{2,1,0:T(2,128)S(1)} %multiply_subtract_fusion.4), channel_id=1, source_target_pairs={{0,4},{4,8},{8,12},{12,16},{16,20},{20,24},{24,28},{1,5},{5,9},{9,... | collective-permute-start | bytes 392 | tf_op jit(solution)/shard_map/ppermute | solution.py:32
  205.5 3.0 collective-permute-start.26
  211.0 4.5 %collective-permute-start.22 = (f32[2,76,6]{2,1,0:T(8,128)S(1)}, f32[2,76,6]{2,1,0:T(8,128)S(1)}, u32[]{:S(2)}, u32[]{:S(2)}) collective-permute-start(f32[2,76,6]{2,1,0:T(8,128)S(1)} %get-tuple-element.100), channel_id=1, source_target_pairs={{0,1},{1,2},{2,3},{4,5},{5,6},{6,7},{8,9},{9,10},{10,11},{12,13},{... | collective-permute-start | bytes 10952 | tf_op jit(solution)/shard_map/ppermute | solution.py:32
  217.4 2.1 divide_exponential_fusion
  219.7 2.1 multiply_add_fusion
  225.3 5.4 %collective-permute-start.28 = (f32[2,3,11]{2,1,0:T(4,128)S(1)}, f32[2,3,11]{2,1,0:T(4,128)S(1)}, u32[]{:S(2)}, u32[]{:S(2)}) collective-permute-start(f32[2,3,11]{2,1,0:T(4,128)S(1)} %get-tuple-element.196), channel_id=1, source_target_pairs={{0,4},{4,8},{8,12},{12,16},{16,20},{20,24},{24,28},{1,5},{5,9},{9,... | collective-permute-start | bytes 800 | tf_op jit(solution)/shard_map/ppermute | solution.py:32
  233.4 4.5 %collective-permute-start.30 = (f32[2,11,3]{2,1,0:T(8,128)S(1)}, f32[2,11,3]{2,1,0:T(8,128)S(1)}, u32[]{:S(2)}, u32[]{:S(2)}) collective-permute-start(f32[2,11,3]{2,1,0:T(8,128)S(1)} %get-tuple-element.184), channel_id=1, source_target_pairs={{0,1},{1,2},{2,3},{4,5},{5,6},{6,7},{8,9},{9,10},{10,11},{12,13},{... | collective-permute-start | bytes 800 | tf_op jit(solution)/shard_map/ppermute | solution.py:32
  241.0 5.7 %collective-permute-start.32 = (f32[2,2,8]{2,1,0:T(2,128)S(1)}, f32[2,2,8]{2,1,0:T(2,128)S(1)}, u32[]{:S(2)}, u32[]{:S(2)}) collective-permute-start(f32[2,2,8]{2,1,0:T(2,128)S(1)} %get-tuple-element.13), channel_id=1, source_target_pairs={{0,4},{4,8},{8,12},{12,16},{16,20},{20,24},{24,28},{1,5},{5,9},{9,... | collective-permute-start | bytes 392 | tf_op jit(solution)/shard_map/ppermute | solution.py:32
  249.3 4.9 %collective-permute-start.34 = (f32[2,6,2]{2,1,0:T(8,128)S(1)}, f32[2,6,2]{2,1,0:T(8,128)S(1)}, u32[]{:S(2)}, u32[]{:S(2)}) collective-permute-start(f32[2,6,2]{2,1,0:T(8,128)S(1)} %get-tuple-element.194), channel_id=1, source_target_pairs={{0,1},{1,2},{2,3},{4,5},{5,6},{6,7},{8,9},{9,10},{10,11},{12,13},{... | collective-permute-start | bytes 296 | tf_op jit(solution)/shard_map/ppermute | solution.py:32
  256.4 47.4 %all-reduce.13 = (f32[]{:T(128)}, f32[]{:T(128)}) all-reduce(f32[]{:T(128)} %get-tuple-element.12, f32[]{:T(128)} %multiply_reduce_fusion.1), channel_id=1, replica_groups=mesh['ty'=8,'tx'=4] {'ty','tx'}, use_global_device_ids=true, to_apply=%region_10.11 | all-reduce | flops 2 | bytes 16 | tf_op jit(solution)/shard_map/psum | solution.py:178
  306.9 4.8 %collective-permute-start.36 = (f32[2,3,11]{2,1,0:T(4,128)S(1)}, f32[2,3,11]{2,1,0:T(4,128)S(1)}, u32[]{:S(2)}, u32[]{:S(2)}) collective-permute-start(f32[2,3,11]{2,1,0:T(4,128)S(1)} %get-tuple-element.192), channel_id=1, source_target_pairs={{0,4},{4,8},{8,12},{12,16},{16,20},{20,24},{24,28},{1,5},{5,9},{9,... | collective-permute-start | bytes 800 | tf_op jit(solution)/shard_map/ppermute | solution.py:32
  314.4 3.0 collective-permute-start.38
  320.5 5.4 %collective-permute-start.40 = (f32[2,2,8]{2,1,0:T(2,128)S(1)}, f32[2,2,8]{2,1,0:T(2,128)S(1)}, u32[]{:S(2)}, u32[]{:S(2)}) collective-permute-start(f32[2,2,8]{2,1,0:T(2,128)S(1)} %get-tuple-element.11), channel_id=1, source_target_pairs={{0,4},{4,8},{8,12},{12,16},{16,20},{20,24},{24,28},{1,5},{5,9},{9,... | collective-permute-start | bytes 392 | tf_op jit(solution)/shard_map/ppermute | solution.py:32
  328.6 3.5 collective-permute-start.42
  334.2 47.2 %all-reduce.12 = (f32[]{:T(128)}, f32[]{:T(128)}) all-reduce(f32[]{:T(128)} %get-tuple-element.10, f32[]{:T(128)} %multiply_reduce_fusion), channel_id=1, replica_groups=mesh['ty'=8,'tx'=4] {'ty','tx'}, use_global_device_ids=true, to_apply=%region_14.15 | all-reduce | flops 2 | bytes 16 | tf_op jit(solution)/shard_map/psum | solution.py:178
  (177 shorter events, 67.6 us)
Async XLA Ops:
  18.3 6.8 %collective-permute-start.1 = (f32[2,6,128]{2,1,0:T(8,128)S(1)}, f32[2,6,128]{2,1,0:T(8,128)S(1)}, u32[]{:S(2)}, u32[]{:S(2)}) collective-permute-start(f32[2,6,128]{2,1,0:T(8,128)S(1)} %get-tuple-element.181), channel_id=1, source_target_pairs={{4,0},{8,4},{12,8},{16,12},{20,16},{24,20},{28,24},{5,1},{9,5},{13... | collective-permute-start | bytes 18440 | tf_op jit(solution)/shard_map/ppermute | solution.py:35
  19.6 6.8 %collective-permute-start = (f32[2,6,128]{2,1,0:T(8,128)S(1)}, f32[2,6,128]{2,1,0:T(8,128)S(1)}, u32[]{:S(2)}, u32[]{:S(2)}) collective-permute-start(f32[2,6,128]{2,1,0:T(8,128)S(1)} %get-tuple-element.180), channel_id=1, source_target_pairs={{0,4},{4,8},{8,12},{12,16},{16,20},{20,24},{24,28},{1,5},{5,9},{9,... | collective-permute-start | bytes 18440 | tf_op jit(solution)/shard_map/ppermute | solution.py:32
  35.3 6.8 %collective-permute-start.5 = (f32[2,3,11]{2,1,0:T(4,128)S(1)}, f32[2,3,11]{2,1,0:T(4,128)S(1)}, u32[]{:S(2)}, u32[]{:S(2)}) collective-permute-start(f32[2,3,11]{2,1,0:T(4,128)S(1)} %get-tuple-element.207), channel_id=1, source_target_pairs={{4,0},{8,4},{12,8},{16,12},{20,16},{24,20},{28,24},{5,1},{9,5},{13... | collective-permute-start | bytes 800 | tf_op jit(solution)/shard_map/ppermute | solution.py:35
  36.6 6.8 %collective-permute-start.4 = (f32[2,3,11]{2,1,0:T(4,128)S(1)}, f32[2,3,11]{2,1,0:T(4,128)S(1)}, u32[]{:S(2)}, u32[]{:S(2)}) collective-permute-start(f32[2,3,11]{2,1,0:T(4,128)S(1)} %get-tuple-element.206), channel_id=1, source_target_pairs={{0,4},{4,8},{8,12},{12,16},{16,20},{20,24},{24,28},{1,5},{5,9},{9,... | collective-permute-start | bytes 800 | tf_op jit(solution)/shard_map/ppermute | solution.py:32
  49.6 7.0 %collective-permute-start.9 = (f32[2,2,8]{2,1,0:T(2,128)S(1)}, f32[2,2,8]{2,1,0:T(2,128)S(1)}, u32[]{:S(2)}, u32[]{:S(2)}) collective-permute-start(f32[2,2,8]{2,1,0:T(2,128)S(1)} %get-tuple-element.36), channel_id=1, source_target_pairs={{4,0},{8,4},{12,8},{16,12},{20,16},{24,20},{28,24},{5,1},{9,5},{13... | collective-permute-start | bytes 392 | tf_op jit(solution)/shard_map/ppermute | solution.py:35
  50.9 7.0 %collective-permute-start.8 = (f32[2,2,8]{2,1,0:T(2,128)S(1)}, f32[2,2,8]{2,1,0:T(2,128)S(1)}, u32[]{:S(2)}, u32[]{:S(2)}) collective-permute-start(f32[2,2,8]{2,1,0:T(2,128)S(1)} %get-tuple-element.36), channel_id=1, source_target_pairs={{0,4},{4,8},{8,12},{12,16},{16,20},{20,24},{24,28},{1,5},{5,9},{9,... | collective-permute-start | bytes 392 | tf_op jit(solution)/shard_map/ppermute | solution.py:32
  58.0 6.2 %collective-permute-start.11 = (f32[2,6,2]{2,1,0:T(8,128)S(1)}, f32[2,6,2]{2,1,0:T(8,128)S(1)}, u32[]{:S(2)}, u32[]{:S(2)}) collective-permute-start(f32[2,6,2]{2,1,0:T(8,128)S(1)} %get-tuple-element.205), channel_id=1, source_target_pairs={{1,0},{2,1},{3,2},{5,4},{6,5},{7,6},{9,8},{10,9},{11,10},{13,12},{... | collective-permute-start | bytes 296 | tf_op jit(solution)/shard_map/ppermute | solution.py:35
  59.2 5.7 %collective-permute-start.10 = (f32[2,6,2]{2,1,0:T(8,128)S(1)}, f32[2,6,2]{2,1,0:T(8,128)S(1)}, u32[]{:S(2)}, u32[]{:S(2)}) collective-permute-start(f32[2,6,2]{2,1,0:T(8,128)S(1)} %get-tuple-element.204), channel_id=1, source_target_pairs={{0,1},{1,2},{2,3},{4,5},{5,6},{6,7},{8,9},{9,10},{10,11},{12,13},{... | collective-permute-start | bytes 296 | tf_op jit(solution)/shard_map/ppermute | solution.py:32
  115.4 12.9 %collective-permute-start.13 = (f32[2,3,11]{2,1,0:T(4,128)S(1)}, f32[2,3,11]{2,1,0:T(4,128)S(1)}, u32[]{:S(2)}, u32[]{:S(2)}) collective-permute-start(f32[2,3,11]{2,1,0:T(4,128)S(1)} %get-tuple-element.203), channel_id=1, source_target_pairs={{4,0},{8,4},{12,8},{16,12},{20,16},{24,20},{28,24},{5,1},{9,5},{13... | collective-permute-start | bytes 800 | tf_op jit(solution)/shard_map/ppermute | solution.py:35
  116.7 11.6 %collective-permute-start.12 = (f32[2,3,11]{2,1,0:T(4,128)S(1)}, f32[2,3,11]{2,1,0:T(4,128)S(1)}, u32[]{:S(2)}, u32[]{:S(2)}) collective-permute-start(f32[2,3,11]{2,1,0:T(4,128)S(1)} %get-tuple-element.202), channel_id=1, source_target_pairs={{0,4},{4,8},{8,12},{12,16},{16,20},{20,24},{24,28},{1,5},{5,9},{9,... | collective-permute-start | bytes 800 | tf_op jit(solution)/shard_map/ppermute | solution.py:32
  121.6 88.0 %collective-permute-start.21 = (f32[2,6,256]{2,1,0:T(8,128)S(1)}, f32[2,6,256]{2,1,0:T(8,128)S(1)}, u32[]{:S(2)}, u32[]{:S(2)}) collective-permute-start(f32[2,6,256]{2,1,0:T(8,128)S(1)} %get-tuple-element.103), channel_id=1, source_target_pairs={{4,0},{8,4},{12,8},{16,12},{20,16},{24,20},{28,24},{5,1},{9,5},{13... | collective-permute-start | bytes 36872 | tf_op jit(solution)/shard_map/ppermute | solution.py:35
  122.9 86.7 %collective-permute-start.20 = (f32[2,6,256]{2,1,0:T(8,128)S(1)}, f32[2,6,256]{2,1,0:T(8,128)S(1)}, u32[]{:S(2)}, u32[]{:S(2)}) collective-permute-start(f32[2,6,256]{2,1,0:T(8,128)S(1)} %get-tuple-element.102), channel_id=1, source_target_pairs={{0,4},{4,8},{8,12},{12,16},{16,20},{20,24},{24,28},{1,5},{5,9},{9,... | collective-permute-start | bytes 36872 | tf_op jit(solution)/shard_map/ppermute | solution.py:32
  134.5 6.8 %collective-permute-start.17 = (f32[2,2,8]{2,1,0:T(2,128)S(1)}, f32[2,2,8]{2,1,0:T(2,128)S(1)}, u32[]{:S(2)}, u32[]{:S(2)}) collective-permute-start(f32[2,2,8]{2,1,0:T(2,128)S(1)} %get-tuple-element.34), channel_id=1, source_target_pairs={{4,0},{8,4},{12,8},{16,12},{20,16},{24,20},{28,24},{5,1},{9,5},{13... | collective-permute-start | bytes 392 | tf_op jit(solution)/shard_map/ppermute | solution.py:35
  135.8 6.7 %collective-permute-start.16 = (f32[2,2,8]{2,1,0:T(2,128)S(1)}, f32[2,2,8]{2,1,0:T(2,128)S(1)}, u32[]{:S(2)}, u32[]{:S(2)}) collective-permute-start(f32[2,2,8]{2,1,0:T(2,128)S(1)} %get-tuple-element.34), channel_id=1, source_target_pairs={{0,4},{4,8},{8,12},{12,16},{16,20},{20,24},{24,28},{1,5},{5,9},{9,... | collective-permute-start | bytes 392 | tf_op jit(solution)/shard_map/ppermute | solution.py:32
  142.6 4.7 %collective-permute-start.19 = (f32[2,6,2]{2,1,0:T(8,128)S(1)}, f32[2,6,2]{2,1,0:T(8,128)S(1)}, u32[]{:S(2)}, u32[]{:S(2)}) collective-permute-start(f32[2,6,2]{2,1,0:T(8,128)S(1)} %get-tuple-element.201), channel_id=1, source_target_pairs={{1,0},{2,1},{3,2},{5,4},{6,5},{7,6},{9,8},{10,9},{11,10},{13,12},{... | collective-permute-start | bytes 296 | tf_op jit(solution)/shard_map/ppermute | solution.py:35
  196.7 6.3 %collective-permute-start.25 = (f32[2,2,8]{2,1,0:T(2,128)S(1)}, f32[2,2,8]{2,1,0:T(2,128)S(1)}, u32[]{:S(2)}, u32[]{:S(2)}) collective-permute-start(f32[2,2,8]{2,1,0:T(2,128)S(1)} %multiply_subtract_fusion.4), channel_id=1, source_target_pairs={{4,0},{8,4},{12,8},{16,12},{20,16},{24,20},{28,24},{5,1},{9,5},{13... | collective-permute-start | bytes 392 | tf_op jit(solution)/shard_map/ppermute | solution.py:35
  198.0 6.1 %collective-permute-start.24 = (f32[2,2,8]{2,1,0:T(2,128)S(1)}, f32[2,2,8]{2,1,0:T(2,128)S(1)}, u32[]{:S(2)}, u32[]{:S(2)}) collective-permute-start(f32[2,2,8]{2,1,0:T(2,128)S(1)} %multiply_subtract_fusion.4), channel_id=1, source_target_pairs={{0,4},{4,8},{8,12},{12,16},{16,20},{20,24},{24,28},{1,5},{5,9},{9,... | collective-permute-start | bytes 392 | tf_op jit(solution)/shard_map/ppermute | solution.py:32
  209.7 6.2 %collective-permute-start.23 = (f32[2,76,6]{2,1,0:T(8,128)S(1)}, f32[2,76,6]{2,1,0:T(8,128)S(1)}, u32[]{:S(2)}, u32[]{:S(2)}) collective-permute-start(f32[2,76,6]{2,1,0:T(8,128)S(1)} %get-tuple-element.101), channel_id=1, source_target_pairs={{1,0},{2,1},{3,2},{5,4},{6,5},{7,6},{9,8},{10,9},{11,10},{13,12},{... | collective-permute-start | bytes 10952 | tf_op jit(solution)/shard_map/ppermute | solution.py:35
  211.0 5.2 %collective-permute-start.22 = (f32[2,76,6]{2,1,0:T(8,128)S(1)}, f32[2,76,6]{2,1,0:T(8,128)S(1)}, u32[]{:S(2)}, u32[]{:S(2)}) collective-permute-start(f32[2,76,6]{2,1,0:T(8,128)S(1)} %get-tuple-element.100), channel_id=1, source_target_pairs={{0,1},{1,2},{2,3},{4,5},{5,6},{6,7},{8,9},{9,10},{10,11},{12,13},{... | collective-permute-start | bytes 10952 | tf_op jit(solution)/shard_map/ppermute | solution.py:32
  224.0 6.7 %collective-permute-start.29 = (f32[2,3,11]{2,1,0:T(4,128)S(1)}, f32[2,3,11]{2,1,0:T(4,128)S(1)}, u32[]{:S(2)}, u32[]{:S(2)}) collective-permute-start(f32[2,3,11]{2,1,0:T(4,128)S(1)} %get-tuple-element.197), channel_id=1, source_target_pairs={{4,0},{8,4},{12,8},{16,12},{20,16},{24,20},{28,24},{5,1},{9,5},{13... | collective-permute-start | bytes 800 | tf_op jit(solution)/shard_map/ppermute | solution.py:35
  225.3 6.7 %collective-permute-start.28 = (f32[2,3,11]{2,1,0:T(4,128)S(1)}, f32[2,3,11]{2,1,0:T(4,128)S(1)}, u32[]{:S(2)}, u32[]{:S(2)}) collective-permute-start(f32[2,3,11]{2,1,0:T(4,128)S(1)} %get-tuple-element.196), channel_id=1, source_target_pairs={{0,4},{4,8},{8,12},{12,16},{16,20},{20,24},{24,28},{1,5},{5,9},{9,... | collective-permute-start | bytes 800 | tf_op jit(solution)/shard_map/ppermute | solution.py:32
  232.1 5.8 %collective-permute-start.31 = (f32[2,11,3]{2,1,0:T(8,128)S(1)}, f32[2,11,3]{2,1,0:T(8,128)S(1)}, u32[]{:S(2)}, u32[]{:S(2)}) collective-permute-start(f32[2,11,3]{2,1,0:T(8,128)S(1)} %get-tuple-element.185), channel_id=1, source_target_pairs={{1,0},{2,1},{3,2},{5,4},{6,5},{7,6},{9,8},{10,9},{11,10},{13,12},{... | collective-permute-start | bytes 800 | tf_op jit(solution)/shard_map/ppermute | solution.py:35
  233.4 5.4 %collective-permute-start.30 = (f32[2,11,3]{2,1,0:T(8,128)S(1)}, f32[2,11,3]{2,1,0:T(8,128)S(1)}, u32[]{:S(2)}, u32[]{:S(2)}) collective-permute-start(f32[2,11,3]{2,1,0:T(8,128)S(1)} %get-tuple-element.184), channel_id=1, source_target_pairs={{0,1},{1,2},{2,3},{4,5},{5,6},{6,7},{8,9},{9,10},{10,11},{12,13},{... | collective-permute-start | bytes 800 | tf_op jit(solution)/shard_map/ppermute | solution.py:32
  239.7 7.0 %collective-permute-start.33 = (f32[2,2,8]{2,1,0:T(2,128)S(1)}, f32[2,2,8]{2,1,0:T(2,128)S(1)}, u32[]{:S(2)}, u32[]{:S(2)}) collective-permute-start(f32[2,2,8]{2,1,0:T(2,128)S(1)} %get-tuple-element.13), channel_id=1, source_target_pairs={{4,0},{8,4},{12,8},{16,12},{20,16},{24,20},{28,24},{5,1},{9,5},{13... | collective-permute-start | bytes 392 | tf_op jit(solution)/shard_map/ppermute | solution.py:35
  241.0 7.0 %collective-permute-start.32 = (f32[2,2,8]{2,1,0:T(2,128)S(1)}, f32[2,2,8]{2,1,0:T(2,128)S(1)}, u32[]{:S(2)}, u32[]{:S(2)}) collective-permute-start(f32[2,2,8]{2,1,0:T(2,128)S(1)} %get-tuple-element.13), channel_id=1, source_target_pairs={{0,4},{4,8},{8,12},{12,16},{16,20},{20,24},{24,28},{1,5},{5,9},{9,... | collective-permute-start | bytes 392 | tf_op jit(solution)/shard_map/ppermute | solution.py:32
  248.1 6.2 %collective-permute-start.35 = (f32[2,6,2]{2,1,0:T(8,128)S(1)}, f32[2,6,2]{2,1,0:T(8,128)S(1)}, u32[]{:S(2)}, u32[]{:S(2)}) collective-permute-start(f32[2,6,2]{2,1,0:T(8,128)S(1)} %get-tuple-element.195), channel_id=1, source_target_pairs={{1,0},{2,1},{3,2},{5,4},{6,5},{7,6},{9,8},{10,9},{11,10},{13,12},{... | collective-permute-start | bytes 296 | tf_op jit(solution)/shard_map/ppermute | solution.py:35
  249.3 5.8 %collective-permute-start.34 = (f32[2,6,2]{2,1,0:T(8,128)S(1)}, f32[2,6,2]{2,1,0:T(8,128)S(1)}, u32[]{:S(2)}, u32[]{:S(2)}) collective-permute-start(f32[2,6,2]{2,1,0:T(8,128)S(1)} %get-tuple-element.194), channel_id=1, source_target_pairs={{0,1},{1,2},{2,3},{4,5},{5,6},{6,7},{8,9},{9,10},{10,11},{12,13},{... | collective-permute-start | bytes 296 | tf_op jit(solution)/shard_map/ppermute | solution.py:32
  305.6 6.1 %collective-permute-start.37 = (f32[2,3,11]{2,1,0:T(4,128)S(1)}, f32[2,3,11]{2,1,0:T(4,128)S(1)}, u32[]{:S(2)}, u32[]{:S(2)}) collective-permute-start(f32[2,3,11]{2,1,0:T(4,128)S(1)} %get-tuple-element.193), channel_id=1, source_target_pairs={{4,0},{8,4},{12,8},{16,12},{20,16},{24,20},{28,24},{5,1},{9,5},{13... | collective-permute-start | bytes 800 | tf_op jit(solution)/shard_map/ppermute | solution.py:35
  306.9 6.1 %collective-permute-start.36 = (f32[2,3,11]{2,1,0:T(4,128)S(1)}, f32[2,3,11]{2,1,0:T(4,128)S(1)}, u32[]{:S(2)}, u32[]{:S(2)}) collective-permute-start(f32[2,3,11]{2,1,0:T(4,128)S(1)} %get-tuple-element.192), channel_id=1, source_target_pairs={{0,4},{4,8},{8,12},{12,16},{16,20},{20,24},{24,28},{1,5},{5,9},{9,... | collective-permute-start | bytes 800 | tf_op jit(solution)/shard_map/ppermute | solution.py:32
  319.2 6.7 %collective-permute-start.41 = (f32[2,2,8]{2,1,0:T(2,128)S(1)}, f32[2,2,8]{2,1,0:T(2,128)S(1)}, u32[]{:S(2)}, u32[]{:S(2)}) collective-permute-start(f32[2,2,8]{2,1,0:T(2,128)S(1)} %get-tuple-element.11), channel_id=1, source_target_pairs={{4,0},{8,4},{12,8},{16,12},{20,16},{24,20},{28,24},{5,1},{9,5},{13... | collective-permute-start | bytes 392 | tf_op jit(solution)/shard_map/ppermute | solution.py:35
  320.5 6.7 %collective-permute-start.40 = (f32[2,2,8]{2,1,0:T(2,128)S(1)}, f32[2,2,8]{2,1,0:T(2,128)S(1)}, u32[]{:S(2)}, u32[]{:S(2)}) collective-permute-start(f32[2,2,8]{2,1,0:T(2,128)S(1)} %get-tuple-element.11), channel_id=1, source_target_pairs={{0,4},{4,8},{8,12},{12,16},{16,20},{20,24},{24,28},{1,5},{5,9},{9,... | collective-permute-start | bytes 392 | tf_op jit(solution)/shard_map/ppermute | solution.py:32
  327.3 4.8 %collective-permute-start.43 = (f32[2,6,2]{2,1,0:T(8,128)S(1)}, f32[2,6,2]{2,1,0:T(8,128)S(1)}, u32[]{:S(2)}, u32[]{:S(2)}) collective-permute-start(f32[2,6,2]{2,1,0:T(8,128)S(1)} %get-tuple-element.191), channel_id=1, source_target_pairs={{1,0},{2,1},{3,2},{5,4},{6,5},{7,6},{9,8},{10,9},{11,10},{13,12},{... | collective-permute-start | bytes 296 | tf_op jit(solution)/shard_map/ppermute | solution.py:35
  (15 other events, 103.5 us)
where the time goes:
time: 386 us; the launch traced here: 384 us
  blocking collectives  188 us (49%)
  starting transfers between devices  128 us (33%)
  waiting for transfers between devices  19.6 us (5%)
  local copies, waits for them, and re-layouts  19.5 us (5%)
  other arithmetic  17.5 us (5%)
  between operations  6.96 us (2%)
  matrix products  4.67 us (1%)
    psum x4, blocking collectives, run_level(): lax.psum((jnp.sum(direction * direction), jnp.sum(curvature_density(summe...  188 us
    ppermute x22, starting transfers between devices, with_halo(): lax.ppermute(lax.slice_in_dim(block, block.shape[dim] - width, None, axis...  99.5 us
    ppermute x22, starting transfers between devices, with_halo(): lax.ppermute(lax.slice_in_dim(block, 0, width, axis=dim), axis, backward)  28.3 us
    ppermute x22, waiting for transfers between devices, with_halo(): lax.ppermute(lax.slice_in_dim(block, block.shape[dim] - width, None, axis...  19.5 us
    another operation x4, local copies, waits for them, and re-layouts, shards(): stacked = jnp.stack([fixed_image, moving_image])  17.6 us
  transfers between devices with their start and end apart: 44, of which 20 were waited for; matrix products, arithmetic and copies ran while one was open for 1% of the time, Pallas kernels for 0%

commit v1 on v0

--- a/solution.py
+++ b/solution.py
@@ -175,9 +175,16 @@
         spilled = with_halo(partial_grad, (("ty", 1), ("tx", 2)), 3)
         direction = fold_rim(fold_rim(spilled, 1, cells_y), 2, cells_x)
         motion = sandwich(rows_window, window_of(direction), cols_window)
-        norm_sum, curvature = lax.psum(
+
+        def _try_all_sums_all(buf, dev_axis, mesh_name):
+            item_now = lax.psum(buf, dev_axis)
+            before = lax.psum(item_now, mesh_name)
+            return before
+
+        norm_sum, curvature = _try_all_sums_all(
             (jnp.sum(direction * direction), jnp.sum(curvature_density(summed, weight, motion))),
-            ("ty", "tx"),
+            "tx",
+            "ty",
         )
         step_size = norm_sum / curvature
         coefficients = coefficients - step_size * direction

time: 386 us -> 320 us (0.83)
  blocking collectives: 188 us -> 128 us
  starting transfers between devices: 128 us -> 123 us
    psum x4 -> x8, blocking collectives: 188 us -> 128 us  [the longest x4 88.5 us: _try_all_sums_all(): before = lax.psum(item_now, mesh_name)]
    ppermute x22, starting transfers between devices: 99.5 us -> 94.5 us  [with_halo(): lax.ppermute(lax.slice_in_dim(block, block.shape[dim] - width, None, axis...]
where the time goes in v1:
time: 320 us; the launch traced here: 319 us
  blocking collectives  128 us (40%)
  starting transfers between devices  123 us (38%)
  waiting for transfers between devices  19.6 us (6%)
  local copies, waits for them, and re-layouts  19.4 us (6%)
  other arithmetic  17.5 us (5%)
  between operations  6.96 us (2%)
  matrix products  4.67 us (1%)
    ppermute x22, starting transfers between devices, with_halo(): lax.ppermute(lax.slice_in_dim(block, block.shape[dim] - width, None, axis...  94.5 us
    psum x4, blocking collectives, _try_all_sums_all(): before = lax.psum(item_now, mesh_name)  88.5 us
    psum x4, blocking collectives, _try_all_sums_all(): item_now = lax.psum(buf, dev_axis)  39.2 us
    ppermute x22, starting transfers between devices, with_halo(): lax.ppermute(lax.slice_in_dim(block, 0, width, axis=dim), axis, backward)  28.3 us
    ppermute x22, waiting for transfers between devices, with_halo(): lax.ppermute(lax.slice_in_dim(block, block.shape[dim] - width, None, axis...  19.5 us
    another operation x4, local copies, waits for them, and re-layouts, shards(): stacked = jnp.stack([fixed_image, moving_image])  17.5 us
  transfers between devices with their start and end apart: 44, of which 20 were waited for; matrix products, arithmetic and copies ran while one was open for 1% of the time, Pallas kernels for 0%

profile of v1, /device:TPU:0, one launch (start us, length us, event | category | flops | bytes accessed | tf_op | source)
XLA Modules:
  0.0 318.6 jit_solution(17011929733056365030)
XLA Ops:
  0.6 6.3 %stack.52 = f32[1,32,2,128,2]{4,3,2,1,0:T(8,128)} reshape(f32[64,256]{1,0:T(8,128)} %param.4) | data formatting | bytes 131072 | tf_op jit(solution)/shard_map/stack | solution.py:196
  9.8 5.5 %stack.51 = f32[1,32,2,128,2]{4,3,2,1,0:T(8,128)} reshape(f32[64,256]{1,0:T(8,128)S(1)} %copy-done.1) | data formatting | bytes 131072 | tf_op jit(solution)/shard_map/stack | solution.py:196
  19.6 5.5 %collective-permute-start = (f32[2,6,128]{2,1,0:T(8,128)S(1)}, f32[2,6,128]{2,1,0:T(8,128)S(1)}, u32[]{:S(2)}, u32[]{:S(2)}) collective-permute-start(f32[2,6,128]{2,1,0:T(8,128)S(1)} %get-tuple-element.188), channel_id=1, source_target_pairs={{0,4},{4,8},{8,12},{12,16},{16,20},{20,24},{24,28},{1,5},{5,9},{9,... | collective-permute-start | bytes 18440 | tf_op jit(solution)/shard_map/ppermute | solution.py:32
  27.8 3.0 collective-permute-start.2
  36.5 5.4 %collective-permute-start.4 = (f32[2,3,11]{2,1,0:T(4,128)S(1)}, f32[2,3,11]{2,1,0:T(4,128)S(1)}, u32[]{:S(2)}, u32[]{:S(2)}) collective-permute-start(f32[2,3,11]{2,1,0:T(4,128)S(1)} %get-tuple-element.214), channel_id=1, source_target_pairs={{0,4},{4,8},{8,12},{12,16},{16,20},{20,24},{24,28},{1,5},{5,9},{9,... | collective-permute-start | bytes 800 | tf_op jit(solution)/shard_map/ppermute | solution.py:32
  44.7 3.1 collective-permute-start.6
  50.8 5.7 %collective-permute-start.8 = (f32[2,2,8]{2,1,0:T(2,128)S(1)}, f32[2,2,8]{2,1,0:T(2,128)S(1)}, u32[]{:S(2)}, u32[]{:S(2)}) collective-permute-start(f32[2,2,8]{2,1,0:T(2,128)S(1)} %get-tuple-element.44), channel_id=1, source_target_pairs={{0,4},{4,8},{8,12},{12,16},{16,20},{20,24},{24,28},{1,5},{5,9},{9,... | collective-permute-start | bytes 392 | tf_op jit(solution)/shard_map/ppermute | solution.py:32
  59.2 4.9 %collective-permute-start.10 = (f32[2,6,2]{2,1,0:T(8,128)S(1)}, f32[2,6,2]{2,1,0:T(8,128)S(1)}, u32[]{:S(2)}, u32[]{:S(2)}) collective-permute-start(f32[2,6,2]{2,1,0:T(8,128)S(1)} %get-tuple-element.212), channel_id=1, source_target_pairs={{0,1},{1,2},{2,3},{4,5},{5,6},{6,7},{8,9},{9,10},{10,11},{12,13},{... | collective-permute-start | bytes 296 | tf_op jit(solution)/shard_map/ppermute | solution.py:32
  66.1 9.7 %all-reduce.19 = (f32[]{:T(128)}, f32[]{:T(128)}) all-reduce(f32[]{:T(128)} %get-tuple-element.43, f32[]{:T(128)} %multiply_reduce_fusion.3), channel_id=1, replica_groups=mesh['ty'=8,'tx'=4] {'tx'}, use_global_device_ids=true, to_apply=%region_2.3 | all-reduce | flops 2 | bytes 16 | tf_op jit(solution)/shard_map/psum | solution.py:180
  75.8 25.2 %all-reduce.15 = (f32[]{:T(128)}, f32[]{:T(128)}) all-reduce(f32[]{:T(128)} %get-tuple-element.16, f32[]{:T(128)} %get-tuple-element.17), channel_id=1, replica_groups=mesh['ty'=8,'tx'=4] {'ty'}, use_global_device_ids=true, to_apply=%region_3.4 | all-reduce | flops 2 | bytes 16 | tf_op jit(solution)/shard_map/psum | solution.py:181
  104.1 4.5 %collective-permute-start.12 = (f32[2,3,11]{2,1,0:T(4,128)S(1)}, f32[2,3,11]{2,1,0:T(4,128)S(1)}, u32[]{:S(2)}, u32[]{:S(2)}) collective-permute-start(f32[2,3,11]{2,1,0:T(4,128)S(1)} %get-tuple-element.210), channel_id=1, source_target_pairs={{0,4},{4,8},{8,12},{12,16},{16,20},{20,24},{24,28},{1,5},{5,9},{9,... | collective-permute-start | bytes 800 | tf_op jit(solution)/shard_map/ppermute | solution.py:32
  110.0 4.5 %collective-permute-start.20 = (f32[2,6,256]{2,1,0:T(8,128)S(1)}, f32[2,6,256]{2,1,0:T(8,128)S(1)}, u32[]{:S(2)}, u32[]{:S(2)}) collective-permute-start(f32[2,6,256]{2,1,0:T(8,128)S(1)} %get-tuple-element.110), channel_id=1, source_target_pairs={{0,4},{4,8},{8,12},{12,16},{16,20},{20,24},{24,28},{1,5},{5,9},{9,... | collective-permute-start | bytes 36872 | tf_op jit(solution)/shard_map/ppermute | solution.py:32
  115.9 3.0 collective-permute-start.14
  122.0 4.5 %collective-permute-start.16 = (f32[2,2,8]{2,1,0:T(2,128)S(1)}, f32[2,2,8]{2,1,0:T(2,128)S(1)}, u32[]{:S(2)}, u32[]{:S(2)}) collective-permute-start(f32[2,2,8]{2,1,0:T(2,128)S(1)} %get-tuple-element.42), channel_id=1, source_target_pairs={{0,4},{4,8},{8,12},{12,16},{16,20},{20,24},{24,28},{1,5},{5,9},{9,... | collective-permute-start | bytes 392 | tf_op jit(solution)/shard_map/ppermute | solution.py:32
  129.2 3.0 collective-permute-start.18
  134.2 9.9 %all-reduce.18 = (f32[]{:T(128)}, f32[]{:T(128)}) all-reduce(f32[]{:T(128)} %get-tuple-element.41, f32[]{:T(128)} %multiply_reduce_fusion.2), channel_id=1, replica_groups=mesh['ty'=8,'tx'=4] {'tx'}, use_global_device_ids=true, to_apply=%region_8.9 | all-reduce | flops 2 | bytes 16 | tf_op jit(solution)/shard_map/psum | solution.py:180
  144.2 20.0 %all-reduce.14 = (f32[]{:T(128)}, f32[]{:T(128)}) all-reduce(f32[]{:T(128)} %get-tuple-element.14, f32[]{:T(128)} %get-tuple-element.15), channel_id=1, replica_groups=mesh['ty'=8,'tx'=4] {'ty'}, use_global_device_ids=true, to_apply=%region_9.10 | all-reduce | flops 2 | bytes 16 | tf_op jit(solution)/shard_map/psum | solution.py:181
  166.9 4.5 %collective-permute-start.24 = (f32[2,2,8]{2,1,0:T(2,128)S(1)}, f32[2,2,8]{2,1,0:T(2,128)S(1)}, u32[]{:S(2)}, u32[]{:S(2)}) collective-permute-start(f32[2,2,8]{2,1,0:T(2,128)S(1)} %multiply_subtract_fusion.4), channel_id=1, source_target_pairs={{0,4},{4,8},{8,12},{12,16},{16,20},{20,24},{24,28},{1,5},{5,9},{9,... | collective-permute-start | bytes 392 | tf_op jit(solution)/shard_map/ppermute | solution.py:32
  174.1 3.0 collective-permute-start.26
  179.6 4.2 %collective-permute-start.22 = (f32[2,76,6]{2,1,0:T(8,128)S(1)}, f32[2,76,6]{2,1,0:T(8,128)S(1)}, u32[]{:S(2)}, u32[]{:S(2)}) collective-permute-start(f32[2,76,6]{2,1,0:T(8,128)S(1)} %get-tuple-element.108), channel_id=1, source_target_pairs={{0,1},{1,2},{2,3},{4,5},{5,6},{6,7},{8,9},{9,10},{10,11},{12,13},{... | collective-permute-start | bytes 10952 | tf_op jit(solution)/shard_map/ppermute | solution.py:32
  193.7 4.8 %collective-permute-start.28 = (f32[2,3,11]{2,1,0:T(4,128)S(1)}, f32[2,3,11]{2,1,0:T(4,128)S(1)}, u32[]{:S(2)}, u32[]{:S(2)}) collective-permute-start(f32[2,3,11]{2,1,0:T(4,128)S(1)} %get-tuple-element.204), channel_id=1, source_target_pairs={{0,4},{4,8},{8,12},{12,16},{16,20},{20,24},{24,28},{1,5},{5,9},{9,... | collective-permute-start | bytes 800 | tf_op jit(solution)/shard_map/ppermute | solution.py:32
  201.2 4.5 %collective-permute-start.30 = (f32[2,11,3]{2,1,0:T(8,128)S(1)}, f32[2,11,3]{2,1,0:T(8,128)S(1)}, u32[]{:S(2)}, u32[]{:S(2)}) collective-permute-start(f32[2,11,3]{2,1,0:T(8,128)S(1)} %get-tuple-element.192), channel_id=1, source_target_pairs={{0,1},{1,2},{2,3},{4,5},{5,6},{6,7},{8,9},{9,10},{10,11},{12,13},{... | collective-permute-start | bytes 800 | tf_op jit(solution)/shard_map/ppermute | solution.py:32
  208.7 5.2 %collective-permute-start.32 = (f32[2,2,8]{2,1,0:T(2,128)S(1)}, f32[2,2,8]{2,1,0:T(2,128)S(1)}, u32[]{:S(2)}, u32[]{:S(2)}) collective-permute-start(f32[2,2,8]{2,1,0:T(2,128)S(1)} %get-tuple-element.21), channel_id=1, source_target_pairs={{0,4},{4,8},{8,12},{12,16},{16,20},{20,24},{24,28},{1,5},{5,9},{9,... | collective-permute-start | bytes 392 | tf_op jit(solution)/shard_map/ppermute | solution.py:32
  216.6 5.2 %collective-permute-start.34 = (f32[2,6,2]{2,1,0:T(8,128)S(1)}, f32[2,6,2]{2,1,0:T(8,128)S(1)}, u32[]{:S(2)}, u32[]{:S(2)}) collective-permute-start(f32[2,6,2]{2,1,0:T(8,128)S(1)} %get-tuple-element.202), channel_id=1, source_target_pairs={{0,1},{1,2},{2,3},{4,5},{5,6},{6,7},{8,9},{9,10},{10,11},{12,13},{... | collective-permute-start | bytes 296 | tf_op jit(solution)/shard_map/ppermute | solution.py:32
  223.9 9.7 %all-reduce.17 = (f32[]{:T(128)}, f32[]{:T(128)}) all-reduce(f32[]{:T(128)} %get-tuple-element.20, f32[]{:T(128)} %multiply_reduce_fusion.1), channel_id=1, replica_groups=mesh['ty'=8,'tx'=4] {'tx'}, use_global_device_ids=true, to_apply=%region_14.15 | all-reduce | flops 2 | bytes 16 | tf_op jit(solution)/shard_map/psum | solution.py:180
  233.6 21.3 %all-reduce.13 = (f32[]{:T(128)}, f32[]{:T(128)}) all-reduce(f32[]{:T(128)} %get-tuple-element.12, f32[]{:T(128)} %get-tuple-element.13), channel_id=1, replica_groups=mesh['ty'=8,'tx'=4] {'ty'}, use_global_device_ids=true, to_apply=%region_15.16 | all-reduce | flops 2 | bytes 16 | tf_op jit(solution)/shard_map/psum | solution.py:181
  258.1 4.5 %collective-permute-start.36 = (f32[2,3,11]{2,1,0:T(4,128)S(1)}, f32[2,3,11]{2,1,0:T(4,128)S(1)}, u32[]{:S(2)}, u32[]{:S(2)}) collective-permute-start(f32[2,3,11]{2,1,0:T(4,128)S(1)} %get-tuple-element.200), channel_id=1, source_target_pairs={{0,4},{4,8},{8,12},{12,16},{16,20},{20,24},{24,28},{1,5},{5,9},{9,... | collective-permute-start | bytes 800 | tf_op jit(solution)/shard_map/ppermute | solution.py:32
  265.3 3.0 collective-permute-start.38
  271.4 4.8 %collective-permute-start.40 = (f32[2,2,8]{2,1,0:T(2,128)S(1)}, f32[2,2,8]{2,1,0:T(2,128)S(1)}, u32[]{:S(2)}, u32[]{:S(2)}) collective-permute-start(f32[2,2,8]{2,1,0:T(2,128)S(1)} %get-tuple-element.19), channel_id=1, source_target_pairs={{0,4},{4,8},{8,12},{12,16},{16,20},{20,24},{24,28},{1,5},{5,9},{9,... | collective-permute-start | bytes 392 | tf_op jit(solution)/shard_map/ppermute | solution.py:32
  278.9 3.2 %collective-permute-start.42 = (f32[2,6,2]{2,1,0:T(8,128)S(1)}, f32[2,6,2]{2,1,0:T(8,128)S(1)}, u32[]{:S(2)}, u32[]{:S(2)}) collective-permute-start(f32[2,6,2]{2,1,0:T(8,128)S(1)} %get-tuple-element.198), channel_id=1, source_target_pairs={{0,1},{1,2},{2,3},{4,5},{5,6},{6,7},{8,9},{9,10},{10,11},{12,13},{... | collective-permute-start | bytes 296 | tf_op jit(solution)/shard_map/ppermute | solution.py:32
  284.2 9.7 %all-reduce.16 = (f32[]{:T(128)}, f32[]{:T(128)}) all-reduce(f32[]{:T(128)} %get-tuple-element.18, f32[]{:T(128)} %multiply_reduce_fusion), channel_id=1, replica_groups=mesh['ty'=8,'tx'=4] {'tx'}, use_global_device_ids=true, to_apply=%region_20.21 | all-reduce | flops 2 | bytes 16 | tf_op jit(solution)/shard_map/psum | solution.py:180
  294.0 22.0 %all-reduce.12 = (f32[]{:T(128)}, f32[]{:T(128)}) all-reduce(f32[]{:T(128)} %get-tuple-element.10, f32[]{:T(128)} %get-tuple-element.11), channel_id=1, replica_groups=mesh['ty'=8,'tx'=4] {'ty'}, use_global_device_ids=true, to_apply=%region_21.22 | all-reduce | flops 2 | bytes 16 | tf_op jit(solution)/shard_map/psum | solution.py:181
  (181 shorter events, 77.6 us)
Async XLA Ops:
  18.3 6.8 %collective-permute-start.1 = (f32[2,6,128]{2,1,0:T(8,128)S(1)}, f32[2,6,128]{2,1,0:T(8,128)S(1)}, u32[]{:S(2)}, u32[]{:S(2)}) collective-permute-start(f32[2,6,128]{2,1,0:T(8,128)S(1)} %get-tuple-element.189), channel_id=1, source_target_pairs={{4,0},{8,4},{12,8},{16,12},{20,16},{24,20},{28,24},{5,1},{9,5},{13... | collective-permute-start | bytes 18440 | tf_op jit(solution)/shard_map/ppermute | solution.py:35
  19.6 6.8 %collective-permute-start = (f32[2,6,128]{2,1,0:T(8,128)S(1)}, f32[2,6,128]{2,1,0:T(8,128)S(1)}, u32[]{:S(2)}, u32[]{:S(2)}) collective-permute-start(f32[2,6,128]{2,1,0:T(8,128)S(1)} %get-tuple-element.188), channel_id=1, source_target_pairs={{0,4},{4,8},{8,12},{12,16},{16,20},{20,24},{24,28},{1,5},{5,9},{9,... | collective-permute-start | bytes 18440 | tf_op jit(solution)/shard_map/ppermute | solution.py:32
  26.5 4.6 %collective-permute-start.3 = (f32[2,44,6]{2,1,0:T(8,128)S(1)}, f32[2,44,6]{2,1,0:T(8,128)S(1)}, u32[]{:S(2)}, u32[]{:S(2)}) collective-permute-start(f32[2,44,6]{2,1,0:T(8,128)S(1)} %get-tuple-element.176), channel_id=1, source_target_pairs={{1,0},{2,1},{3,2},{5,4},{6,5},{7,6},{9,8},{10,9},{11,10},{13,12},{... | collective-permute-start | bytes 6344 | tf_op jit(solution)/shard_map/ppermute | solution.py:35
  35.2 6.8 %collective-permute-start.5 = (f32[2,3,11]{2,1,0:T(4,128)S(1)}, f32[2,3,11]{2,1,0:T(4,128)S(1)}, u32[]{:S(2)}, u32[]{:S(2)}) collective-permute-start(f32[2,3,11]{2,1,0:T(4,128)S(1)} %get-tuple-element.215), channel_id=1, source_target_pairs={{4,0},{8,4},{12,8},{16,12},{20,16},{24,20},{28,24},{5,1},{9,5},{13... | collective-permute-start | bytes 800 | tf_op jit(solution)/shard_map/ppermute | solution.py:35
  36.5 6.8 %collective-permute-start.4 = (f32[2,3,11]{2,1,0:T(4,128)S(1)}, f32[2,3,11]{2,1,0:T(4,128)S(1)}, u32[]{:S(2)}, u32[]{:S(2)}) collective-permute-start(f32[2,3,11]{2,1,0:T(4,128)S(1)} %get-tuple-element.214), channel_id=1, source_target_pairs={{0,4},{4,8},{8,12},{12,16},{16,20},{20,24},{24,28},{1,5},{5,9},{9,... | collective-permute-start | bytes 800 | tf_op jit(solution)/shard_map/ppermute | solution.py:32
  49.5 7.0 %collective-permute-start.9 = (f32[2,2,8]{2,1,0:T(2,128)S(1)}, f32[2,2,8]{2,1,0:T(2,128)S(1)}, u32[]{:S(2)}, u32[]{:S(2)}) collective-permute-start(f32[2,2,8]{2,1,0:T(2,128)S(1)} %get-tuple-element.44), channel_id=1, source_target_pairs={{4,0},{8,4},{12,8},{16,12},{20,16},{24,20},{28,24},{5,1},{9,5},{13... | collective-permute-start | bytes 392 | tf_op jit(solution)/shard_map/ppermute | solution.py:35
  50.8 7.0 %collective-permute-start.8 = (f32[2,2,8]{2,1,0:T(2,128)S(1)}, f32[2,2,8]{2,1,0:T(2,128)S(1)}, u32[]{:S(2)}, u32[]{:S(2)}) collective-permute-start(f32[2,2,8]{2,1,0:T(2,128)S(1)} %get-tuple-element.44), channel_id=1, source_target_pairs={{0,4},{4,8},{8,12},{12,16},{16,20},{20,24},{24,28},{1,5},{5,9},{9,... | collective-permute-start | bytes 392 | tf_op jit(solution)/shard_map/ppermute | solution.py:32
  57.9 6.2 %collective-permute-start.11 = (f32[2,6,2]{2,1,0:T(8,128)S(1)}, f32[2,6,2]{2,1,0:T(8,128)S(1)}, u32[]{:S(2)}, u32[]{:S(2)}) collective-permute-start(f32[2,6,2]{2,1,0:T(8,128)S(1)} %get-tuple-element.213), channel_id=1, source_target_pairs={{1,0},{2,1},{3,2},{5,4},{6,5},{7,6},{9,8},{10,9},{11,10},{13,12},{... | collective-permute-start | bytes 296 | tf_op jit(solution)/shard_map/ppermute | solution.py:35
  59.2 5.7 %collective-permute-start.10 = (f32[2,6,2]{2,1,0:T(8,128)S(1)}, f32[2,6,2]{2,1,0:T(8,128)S(1)}, u32[]{:S(2)}, u32[]{:S(2)}) collective-permute-start(f32[2,6,2]{2,1,0:T(8,128)S(1)} %get-tuple-element.212), channel_id=1, source_target_pairs={{0,1},{1,2},{2,3},{4,5},{5,6},{6,7},{8,9},{9,10},{10,11},{12,13},{... | collective-permute-start | bytes 296 | tf_op jit(solution)/shard_map/ppermute | solution.py:32
  102.8 11.7 %collective-permute-start.13 = (f32[2,3,11]{2,1,0:T(4,128)S(1)}, f32[2,3,11]{2,1,0:T(4,128)S(1)}, u32[]{:S(2)}, u32[]{:S(2)}) collective-permute-start(f32[2,3,11]{2,1,0:T(4,128)S(1)} %get-tuple-element.211), channel_id=1, source_target_pairs={{4,0},{8,4},{12,8},{16,12},{20,16},{24,20},{28,24},{5,1},{9,5},{13... | collective-permute-start | bytes 800 | tf_op jit(solution)/shard_map/ppermute | solution.py:35
  104.1 10.4 %collective-permute-start.12 = (f32[2,3,11]{2,1,0:T(4,128)S(1)}, f32[2,3,11]{2,1,0:T(4,128)S(1)}, u32[]{:S(2)}, u32[]{:S(2)}) collective-permute-start(f32[2,3,11]{2,1,0:T(4,128)S(1)} %get-tuple-element.210), channel_id=1, source_target_pairs={{0,4},{4,8},{8,12},{12,16},{16,20},{20,24},{24,28},{1,5},{5,9},{9,... | collective-permute-start | bytes 800 | tf_op jit(solution)/shard_map/ppermute | solution.py:32
  108.7 69.5 %collective-permute-start.21 = (f32[2,6,256]{2,1,0:T(8,128)S(1)}, f32[2,6,256]{2,1,0:T(8,128)S(1)}, u32[]{:S(2)}, u32[]{:S(2)}) collective-permute-start(f32[2,6,256]{2,1,0:T(8,128)S(1)} %get-tuple-element.111), channel_id=1, source_target_pairs={{4,0},{8,4},{12,8},{16,12},{20,16},{24,20},{28,24},{5,1},{9,5},{13... | collective-permute-start | bytes 36872 | tf_op jit(solution)/shard_map/ppermute | solution.py:35
  110.0 68.2 %collective-permute-start.20 = (f32[2,6,256]{2,1,0:T(8,128)S(1)}, f32[2,6,256]{2,1,0:T(8,128)S(1)}, u32[]{:S(2)}, u32[]{:S(2)}) collective-permute-start(f32[2,6,256]{2,1,0:T(8,128)S(1)} %get-tuple-element.110), channel_id=1, source_target_pairs={{0,4},{4,8},{8,12},{12,16},{16,20},{20,24},{24,28},{1,5},{5,9},{9,... | collective-permute-start | bytes 36872 | tf_op jit(solution)/shard_map/ppermute | solution.py:32
  120.7 5.9 %collective-permute-start.17 = (f32[2,2,8]{2,1,0:T(2,128)S(1)}, f32[2,2,8]{2,1,0:T(2,128)S(1)}, u32[]{:S(2)}, u32[]{:S(2)}) collective-permute-start(f32[2,2,8]{2,1,0:T(2,128)S(1)} %get-tuple-element.42), channel_id=1, source_target_pairs={{4,0},{8,4},{12,8},{16,12},{20,16},{24,20},{28,24},{5,1},{9,5},{13... | collective-permute-start | bytes 392 | tf_op jit(solution)/shard_map/ppermute | solution.py:35
  122.0 5.8 %collective-permute-start.16 = (f32[2,2,8]{2,1,0:T(2,128)S(1)}, f32[2,2,8]{2,1,0:T(2,128)S(1)}, u32[]{:S(2)}, u32[]{:S(2)}) collective-permute-start(f32[2,2,8]{2,1,0:T(2,128)S(1)} %get-tuple-element.42), channel_id=1, source_target_pairs={{0,4},{4,8},{8,12},{12,16},{16,20},{20,24},{24,28},{1,5},{5,9},{9,... | collective-permute-start | bytes 392 | tf_op jit(solution)/shard_map/ppermute | solution.py:32
  165.6 6.1 %collective-permute-start.25 = (f32[2,2,8]{2,1,0:T(2,128)S(1)}, f32[2,2,8]{2,1,0:T(2,128)S(1)}, u32[]{:S(2)}, u32[]{:S(2)}) collective-permute-start(f32[2,2,8]{2,1,0:T(2,128)S(1)} %multiply_subtract_fusion.4), channel_id=1, source_target_pairs={{4,0},{8,4},{12,8},{16,12},{20,16},{24,20},{28,24},{5,1},{9,5},{13... | collective-permute-start | bytes 392 | tf_op jit(solution)/shard_map/ppermute | solution.py:35
  166.9 5.8 %collective-permute-start.24 = (f32[2,2,8]{2,1,0:T(2,128)S(1)}, f32[2,2,8]{2,1,0:T(2,128)S(1)}, u32[]{:S(2)}, u32[]{:S(2)}) collective-permute-start(f32[2,2,8]{2,1,0:T(2,128)S(1)} %multiply_subtract_fusion.4), channel_id=1, source_target_pairs={{0,4},{4,8},{8,12},{12,16},{16,20},{20,24},{24,28},{1,5},{5,9},{9,... | collective-permute-start | bytes 392 | tf_op jit(solution)/shard_map/ppermute | solution.py:32
  178.3 5.9 %collective-permute-start.23 = (f32[2,76,6]{2,1,0:T(8,128)S(1)}, f32[2,76,6]{2,1,0:T(8,128)S(1)}, u32[]{:S(2)}, u32[]{:S(2)}) collective-permute-start(f32[2,76,6]{2,1,0:T(8,128)S(1)} %get-tuple-element.109), channel_id=1, source_target_pairs={{1,0},{2,1},{3,2},{5,4},{6,5},{7,6},{9,8},{10,9},{11,10},{13,12},{... | collective-permute-start | bytes 10952 | tf_op jit(solution)/shard_map/ppermute | solution.py:35
  179.6 4.9 %collective-permute-start.22 = (f32[2,76,6]{2,1,0:T(8,128)S(1)}, f32[2,76,6]{2,1,0:T(8,128)S(1)}, u32[]{:S(2)}, u32[]{:S(2)}) collective-permute-start(f32[2,76,6]{2,1,0:T(8,128)S(1)} %get-tuple-element.108), channel_id=1, source_target_pairs={{0,1},{1,2},{2,3},{4,5},{5,6},{6,7},{8,9},{9,10},{10,11},{12,13},{... | collective-permute-start | bytes 10952 | tf_op jit(solution)/shard_map/ppermute | solution.py:32
  192.4 6.1 %collective-permute-start.29 = (f32[2,3,11]{2,1,0:T(4,128)S(1)}, f32[2,3,11]{2,1,0:T(4,128)S(1)}, u32[]{:S(2)}, u32[]{:S(2)}) collective-permute-start(f32[2,3,11]{2,1,0:T(4,128)S(1)} %get-tuple-element.205), channel_id=1, source_target_pairs={{4,0},{8,4},{12,8},{16,12},{20,16},{24,20},{28,24},{5,1},{9,5},{13... | collective-permute-start | bytes 800 | tf_op jit(solution)/shard_map/ppermute | solution.py:35
  193.7 6.1 %collective-permute-start.28 = (f32[2,3,11]{2,1,0:T(4,128)S(1)}, f32[2,3,11]{2,1,0:T(4,128)S(1)}, u32[]{:S(2)}, u32[]{:S(2)}) collective-permute-start(f32[2,3,11]{2,1,0:T(4,128)S(1)} %get-tuple-element.204), channel_id=1, source_target_pairs={{0,4},{4,8},{8,12},{12,16},{16,20},{20,24},{24,28},{1,5},{5,9},{9,... | collective-permute-start | bytes 800 | tf_op jit(solution)/shard_map/ppermute | solution.py:32
  199.9 5.8 %collective-permute-start.31 = (f32[2,11,3]{2,1,0:T(8,128)S(1)}, f32[2,11,3]{2,1,0:T(8,128)S(1)}, u32[]{:S(2)}, u32[]{:S(2)}) collective-permute-start(f32[2,11,3]{2,1,0:T(8,128)S(1)} %get-tuple-element.193), channel_id=1, source_target_pairs={{1,0},{2,1},{3,2},{5,4},{6,5},{7,6},{9,8},{10,9},{11,10},{13,12},{... | collective-permute-start | bytes 800 | tf_op jit(solution)/shard_map/ppermute | solution.py:35
  201.2 5.4 %collective-permute-start.30 = (f32[2,11,3]{2,1,0:T(8,128)S(1)}, f32[2,11,3]{2,1,0:T(8,128)S(1)}, u32[]{:S(2)}, u32[]{:S(2)}) collective-permute-start(f32[2,11,3]{2,1,0:T(8,128)S(1)} %get-tuple-element.192), channel_id=1, source_target_pairs={{0,1},{1,2},{2,3},{4,5},{5,6},{6,7},{8,9},{9,10},{10,11},{12,13},{... | collective-permute-start | bytes 800 | tf_op jit(solution)/shard_map/ppermute | solution.py:32
  207.4 6.5 %collective-permute-start.33 = (f32[2,2,8]{2,1,0:T(2,128)S(1)}, f32[2,2,8]{2,1,0:T(2,128)S(1)}, u32[]{:S(2)}, u32[]{:S(2)}) collective-permute-start(f32[2,2,8]{2,1,0:T(2,128)S(1)} %get-tuple-element.21), channel_id=1, source_target_pairs={{4,0},{8,4},{12,8},{16,12},{20,16},{24,20},{28,24},{5,1},{9,5},{13... | collective-permute-start | bytes 392 | tf_op jit(solution)/shard_map/ppermute | solution.py:35
  208.7 6.5 %collective-permute-start.32 = (f32[2,2,8]{2,1,0:T(2,128)S(1)}, f32[2,2,8]{2,1,0:T(2,128)S(1)}, u32[]{:S(2)}, u32[]{:S(2)}) collective-permute-start(f32[2,2,8]{2,1,0:T(2,128)S(1)} %get-tuple-element.21), channel_id=1, source_target_pairs={{0,4},{4,8},{8,12},{12,16},{16,20},{20,24},{24,28},{1,5},{5,9},{9,... | collective-permute-start | bytes 392 | tf_op jit(solution)/shard_map/ppermute | solution.py:32
  215.3 6.5 %collective-permute-start.35 = (f32[2,6,2]{2,1,0:T(8,128)S(1)}, f32[2,6,2]{2,1,0:T(8,128)S(1)}, u32[]{:S(2)}, u32[]{:S(2)}) collective-permute-start(f32[2,6,2]{2,1,0:T(8,128)S(1)} %get-tuple-element.203), channel_id=1, source_target_pairs={{1,0},{2,1},{3,2},{5,4},{6,5},{7,6},{9,8},{10,9},{11,10},{13,12},{... | collective-permute-start | bytes 296 | tf_op jit(solution)/shard_map/ppermute | solution.py:35
  216.6 6.0 %collective-permute-start.34 = (f32[2,6,2]{2,1,0:T(8,128)S(1)}, f32[2,6,2]{2,1,0:T(8,128)S(1)}, u32[]{:S(2)}, u32[]{:S(2)}) collective-permute-start(f32[2,6,2]{2,1,0:T(8,128)S(1)} %get-tuple-element.202), channel_id=1, source_target_pairs={{0,1},{1,2},{2,3},{4,5},{5,6},{6,7},{8,9},{9,10},{10,11},{12,13},{... | collective-permute-start | bytes 296 | tf_op jit(solution)/shard_map/ppermute | solution.py:32
  256.8 5.9 %collective-permute-start.37 = (f32[2,3,11]{2,1,0:T(4,128)S(1)}, f32[2,3,11]{2,1,0:T(4,128)S(1)}, u32[]{:S(2)}, u32[]{:S(2)}) collective-permute-start(f32[2,3,11]{2,1,0:T(4,128)S(1)} %get-tuple-element.201), channel_id=1, source_target_pairs={{4,0},{8,4},{12,8},{16,12},{20,16},{24,20},{28,24},{5,1},{9,5},{13... | collective-permute-start | bytes 800 | tf_op jit(solution)/shard_map/ppermute | solution.py:35
  258.1 5.9 %collective-permute-start.36 = (f32[2,3,11]{2,1,0:T(4,128)S(1)}, f32[2,3,11]{2,1,0:T(4,128)S(1)}, u32[]{:S(2)}, u32[]{:S(2)}) collective-permute-start(f32[2,3,11]{2,1,0:T(4,128)S(1)} %get-tuple-element.200), channel_id=1, source_target_pairs={{0,4},{4,8},{8,12},{12,16},{16,20},{20,24},{24,28},{1,5},{5,9},{9,... | collective-permute-start | bytes 800 | tf_op jit(solution)/shard_map/ppermute | solution.py:32
  270.1 6.1 %collective-permute-start.41 = (f32[2,2,8]{2,1,0:T(2,128)S(1)}, f32[2,2,8]{2,1,0:T(2,128)S(1)}, u32[]{:S(2)}, u32[]{:S(2)}) collective-permute-start(f32[2,2,8]{2,1,0:T(2,128)S(1)} %get-tuple-element.19), channel_id=1, source_target_pairs={{4,0},{8,4},{12,8},{16,12},{20,16},{24,20},{28,24},{5,1},{9,5},{13... | collective-permute-start | bytes 392 | tf_op jit(solution)/shard_map/ppermute | solution.py:35
  271.4 6.1 %collective-permute-start.40 = (f32[2,2,8]{2,1,0:T(2,128)S(1)}, f32[2,2,8]{2,1,0:T(2,128)S(1)}, u32[]{:S(2)}, u32[]{:S(2)}) collective-permute-start(f32[2,2,8]{2,1,0:T(2,128)S(1)} %get-tuple-element.19), channel_id=1, source_target_pairs={{0,4},{4,8},{8,12},{12,16},{16,20},{20,24},{24,28},{1,5},{5,9},{9,... | collective-permute-start | bytes 392 | tf_op jit(solution)/shard_map/ppermute | solution.py:32
  277.6 4.5 %collective-permute-start.43 = (f32[2,6,2]{2,1,0:T(8,128)S(1)}, f32[2,6,2]{2,1,0:T(8,128)S(1)}, u32[]{:S(2)}, u32[]{:S(2)}) collective-permute-start(f32[2,6,2]{2,1,0:T(8,128)S(1)} %get-tuple-element.199), channel_id=1, source_target_pairs={{1,0},{2,1},{3,2},{5,4},{6,5},{7,6},{9,8},{10,9},{11,10},{13,12},{... | collective-permute-start | bytes 296 | tf_op jit(solution)/shard_map/ppermute | solution.py:35
  (15 other events, 102.6 us)
